TPU v7x, 32 devices: a whole 2x2x4 slice. The times are simulated.
32 devices in a mesh: groups: 2 (over x), cells: 16 (over z, y, core).
Axes of the slice: x: 2, y: 2, z: 4, core: 2. Of those that a mesh axis runs over, the one named last changes fastest.
Arguments:
- jacobian: bfloat16 [7, 9, 128, 32, 256], P(None, None, ('groups', 'cells')), parts along dimension 2, may hold values from -1.625 to 12, as said below
- right_side: float32 [3, 128, 32, 256], P(None, ('groups', 'cells')), parts along dimension 1, may hold values from -108 to 108
- scales: float32 [3, 128, 32, 256], P(None, ('groups', 'cells')), parts along dimension 1, may hold values from 0.5 to 2
- weights: float32 [3, 128, 32, 256], P(None, ('groups', 'cells')), parts along dimension 1, may hold values from 0.5 to 2
- aggregate_of: int32 [128, 32, 256], P(('groups', 'cells')), parts along dimension 0, may hold values from 0 to 255, as said below
Outputs:
- solution: float32 [3, 128, 32, 256], P(None, ('groups', 'cells')), parts along dimension 1
- residual: float32 [3, 128, 32, 256], P(None, ('groups', 'cells')), parts along dimension 1
There are 2 independent parts, one for each index of `groups`. A program takes and returns all parts, laid end to end along the dimension named above; each array names one. Nothing has to cross between parts.
Inputs may be any that keep to these rules, and one draw needn't show every extreme that they name: In every block jacobian[k] the first column's entries of the neighbours (k >= 1) are negative, and for each row r the entry jacobian[0, 3 r] exceeds the sum of the magnitudes of jacobian[k, 3 r] over k = 1..6; each cell's own 3 x 3 block is diagonally dominant by rows. `aggregate_of`: every aggregate of 0 to 255 holds cells in every slab. Aggregate a covers base box row a // 32 and column a % 32; the cell in grid row y and column x belongs to an aggregate whose box row is one of (y - 1) // 4, y // 4, (y + 1) // 4 and whose box column is one of (x - 1) // 8, x // 8, (x + 1) // 8, within the grid.
All inputs are finite; a program needn't handle non-finite values.
Results may differ from a plain program's by a relative error of at most 0.0003.
Values sent between devices are 32-bit elements; how exact they have to be, the bound alone decides.
A program may use at most 192 MiB of HBM per device.

v0:
```python
import jax
import jax.numpy as jnp
from jax import lax
from jax.sharding import PartitionSpec as P

GX = 256
AY = 4
AX = 8


DAMPING = 2.0 / 3.0
PRECISE = lax.Precision.HIGHEST
OFFSETS = [(-1, -1), (-1, 0), (-1, 1), (0, -1), (0, 0), (0, 1), (1, -1), (1, 0), (1, 1)]


def padded_2(block, sides, width):
    for axis, dim in sides:
        count = lax.axis_size(axis)
        forward = [(i, i + 1) for i in range(count - 1)]
        backward = [(target, source) for source, target in forward]
        low = lax.ppermute(
            lax.slice_in_dim(block, block.shape[dim] - width, None, axis=dim), axis, forward
        )
        high = lax.ppermute(lax.slice_in_dim(block, 0, width, axis=dim), axis, backward)
        block = jnp.concatenate([low, block, high], axis=dim)
    return block


def neighbour_views(padded):
    return [
        padded[..., 1:-1, 1:-1, 1:-1],
        padded[..., :-2, 1:-1, 1:-1],
        padded[..., 2:, 1:-1, 1:-1],
        padded[..., 1:-1, :-2, 1:-1],
        padded[..., 1:-1, 2:, 1:-1],
        padded[..., 1:-1, 1:-1, :-2],
        padded[..., 1:-1, 1:-1, 2:],
    ]


def stencil_sum(pressure_coef, padded):
    shifted = neighbour_views(padded)
    summed = pressure_coef[0] * shifted[0]
    for way_index in range(1, 7):
        summed = summed + pressure_coef[way_index] * shifted[way_index]
    return summed


def block_product(jacobian, scales, padded):
    shifted = neighbour_views(padded)
    rows_out = []
    for row_index in range(3):
        summed = jnp.zeros(shifted[0].shape[1:], jnp.float32)
        for way_index in range(7):
            for comp_index in range(3):
                block_entry = jacobian[way_index, 3 * row_index + comp_index].astype(jnp.float32)
                summed = summed + block_entry * shifted[way_index][comp_index]
        rows_out.append(scales[row_index] * summed)
    return jnp.stack(rows_out)


def pressure_terms(jacobian, scales, weights):
    coef_list = []
    for way_index in range(7):
        summed = weights[0] * scales[0] * jacobian[way_index, 0].astype(jnp.float32)
        for row_index in range(1, 3):
            summed = summed + weights[row_index] * scales[row_index] * jacobian[
                way_index, 3 * row_index
            ].astype(jnp.float32)
        coef_list.append(summed)
    return jnp.stack(coef_list)


def block_solve(jacobian, values_in):
    mat = [jacobian[0, idx_entry].astype(jnp.float32) for idx_entry in range(9)]
    co_aa = mat[4] * mat[8] - mat[5] * mat[7]
    co_ab = -(mat[3] * mat[8] - mat[5] * mat[6])
    co_ac = mat[3] * mat[7] - mat[4] * mat[6]
    co_ba = -(mat[1] * mat[8] - mat[2] * mat[7])
    co_bb = mat[0] * mat[8] - mat[2] * mat[6]
    co_bc = -(mat[0] * mat[7] - mat[1] * mat[6])
    co_ca = mat[1] * mat[5] - mat[2] * mat[4]
    co_cb = -(mat[0] * mat[5] - mat[2] * mat[3])
    co_cc = mat[0] * mat[4] - mat[1] * mat[3]
    determinant = mat[0] * co_aa + mat[1] * co_ab + mat[2] * co_ac
    first_out = (co_aa * values_in[0] + co_ba * values_in[1] + co_ca * values_in[2]) / determinant
    second_out = (co_ab * values_in[0] + co_bb * values_in[1] + co_cb * values_in[2]) / determinant
    third_out = (co_ac * values_in[0] + co_bc * values_in[1] + co_cc * values_in[2]) / determinant
    return jnp.stack([first_out, second_out, third_out])


def box_layout(field):
    layer_count, row_count, col_count = field.shape
    split = field.reshape(layer_count, row_count // AY, AY, col_count // AX, AX)
    return split.transpose(0, 2, 4, 1, 3).reshape(
        layer_count * AY * AX, row_count // AY * (col_count // AX)
    )


def cell_layout(boxed, layer_count, row_count, col_count):
    split = boxed.reshape(layer_count, AY, AX, row_count // AY, col_count // AX)
    return split.transpose(0, 3, 1, 4, 2).reshape(layer_count, row_count, col_count)


def shift_place(values, row_step, col_step):
    row_count, col_count = values.shape
    padded = jnp.pad(values, 1)
    return padded[1 - row_step : 1 - row_step + row_count, 1 - col_step : 1 - col_step + col_count]


def shift_read(values, row_step, col_step):
    row_count, col_count = values.shape
    padded = jnp.pad(values, 1)
    return padded[1 + row_step : 1 + row_step + row_count, 1 + col_step : 1 + col_step + col_count]


def offset_masks(ids_box):
    across = GX // AX
    box_count = ids_box.shape[1]
    box_index = lax.broadcasted_iota(jnp.int32, (1, box_count), 1)
    base_row = box_index // across
    base_col = box_index % across
    agg_row = ids_box // across
    agg_col = ids_box % across
    present = ids_box >= 0
    return jnp.stack(
        [
            (present & (agg_row - base_row == row_step) & (agg_col - base_col == col_step)).astype(
                jnp.float32
            )
            for row_step, col_step in OFFSETS
        ]
    )


def tile_bands(own_ids, pairs):
    across = GX // AX
    band_rows = own_ids.shape[1] // AY
    own_box = box_layout(own_ids)
    own_masks = offset_masks(own_box)
    own_row = own_box // across
    own_col = own_box % across
    boxed = []
    for near_ids, coef_field in pairs:
        near_box = box_layout(near_ids)
        boxed.append(
            (
                near_box >= 0,
                near_box // across - own_row,
                near_box % across - own_col,
                box_layout(coef_field),
            )
        )
    weighted = []
    for row_step, col_step in OFFSETS:
        running = jnp.zeros(own_box.shape, jnp.float32)
        for present, row_gap, col_gap, coef_box in boxed:
            running = running + jnp.where(
                present & (row_gap == row_step) & (col_gap == col_step), coef_box, 0.0
            )
        weighted.append(running)
    products = jnp.einsum("ocb,dcb->odb", own_masks, jnp.stack(weighted), precision=PRECISE)
    bands = []
    for delta_index in range(9):
        running = jnp.zeros((band_rows, across), jnp.float32)
        for own_index, (row_step, col_step) in enumerate(OFFSETS):
            running = running + shift_place(
                products[own_index, delta_index].reshape(band_rows, across), row_step, col_step
            )
        bands.append(running)
    return jnp.stack(bands)


def restrict_sum(masks, field):
    across = GX // AX
    band_rows = field.shape[1] // AY
    per_offset = jnp.einsum("ocb,cb->ob", masks, box_layout(field), precision=PRECISE)
    running = jnp.zeros((band_rows, across), jnp.float32)
    for own_index, (row_step, col_step) in enumerate(OFFSETS):
        running = running + shift_place(
            per_offset[own_index].reshape(band_rows, across), row_step, col_step
        )
    return running


def prolong(masks, coarse, layer_count, row_count, col_count):
    running = jnp.zeros(masks.shape[1:], jnp.float32)
    for own_index, (row_step, col_step) in enumerate(OFFSETS):
        running = running + masks[own_index] * shift_read(coarse, row_step, col_step).reshape(1, -1)
    return cell_layout(running, layer_count, row_count, col_count)


def band_apply(bands, values):
    running = jnp.zeros(values.shape, jnp.float32)
    for delta_index, (row_step, col_step) in enumerate(OFFSETS):
        running = running + bands[delta_index] * shift_read(values, row_step, col_step)
    return running


def bordered_apply(pressure_coef, bordered):
    return stencil_sum(pressure_coef, jnp.pad(bordered, ((0, 0), (1, 1), (1, 1))))


def smooth_apply(pressure_coef, values_in):
    bordered = padded_2(values_in, (("cells", 0),), 1)
    return bordered_apply(pressure_coef, bordered)


def pressure_apply(pressure_coef, values_in):
    bordered = padded_2(values_in, (("cells", 0),), 1)
    return bordered_apply(pressure_coef, bordered)


def field_apply(jacobian, scales, values_in):
    bordered = padded_2(values_in, (("cells", 1),), 1)
    return block_product(jacobian, scales, jnp.pad(bordered, ((0, 0), (0, 0), (1, 1), (1, 1))))


def coarse_apply(self_bands, lower_bands, upper_bands, coarse):
    bordered = padded_2(coarse[None], (("cells", 0),), 1)
    summed = band_apply(self_bands, coarse)
    summed = summed + band_apply(lower_bands, bordered[0])
    return summed + band_apply(upper_bands, bordered[2])


def shards(jacobian, right_side, scales, weights, aggregate_of):
    layer_count, row_count, col_count = aggregate_of.shape
    pressure_coef = pressure_terms(jacobian, scales, weights)
    bordered_ids = padded_2(aggregate_of + 1, (("cells", 0),), 1)
    near_views = neighbour_views(jnp.pad(bordered_ids, ((0, 0), (1, 1), (1, 1))))
    near_ids = [view - 1 for view in near_views]
    depth = lax.broadcasted_iota(jnp.int32, (layer_count, 1, 1), 0)
    keep_lower = (depth >= 1).astype(jnp.float32)
    keep_upper = (depth <= layer_count - 2).astype(jnp.float32)
    keeps = [1.0, keep_lower, keep_upper, 1.0, 1.0, 1.0, 1.0]
    self_pairs = [
        (near_ids[way_index], pressure_coef[way_index] * keeps[way_index]) for way_index in range(7)
    ]
    self_bands = tile_bands(aggregate_of, self_pairs)
    lower_bands = tile_bands(aggregate_of[:1], [(near_ids[1][:1], pressure_coef[1][:1])])
    upper_bands = tile_bands(aggregate_of[-1:], [(near_ids[2][-1:], pressure_coef[2][-1:])])
    slab_masks = offset_masks(box_layout(aggregate_of))
    coarse_diag = self_bands[4]
    main_local = jnp.sum(self_bands).reshape(1)
    lower_local = jnp.sum(lower_bands).reshape(1)
    upper_local = jnp.sum(upper_bands).reshape(1)
    side_norm = jnp.sqrt(lax.psum(jnp.sum(right_side * right_side), "cells") + 1e-06)
    krylov_basis = right_side / side_norm
    restricted = (
        weights[0] * krylov_basis[0] + weights[1] * krylov_basis[1] + weights[2] * krylov_basis[2]
    )
    diag_fine = pressure_coef[0]
    first_iterate = DAMPING * restricted / diag_fine
    second_iterate = (
        first_iterate
        + DAMPING * (restricted - smooth_apply(pressure_coef, first_iterate)) / diag_fine
    )
    fine_residual = restricted - smooth_apply(pressure_coef, second_iterate)
    coarse_rhs = restrict_sum(slab_masks, fine_residual)
    coarse_first = DAMPING * coarse_rhs / coarse_diag
    coarse_residual = coarse_rhs - coarse_apply(self_bands, lower_bands, upper_bands, coarse_first)
    slab_residual = jnp.sum(coarse_residual).reshape(1)
    main_all, lower_all, upper_all, residual_all = (
        lax.all_gather(main_local, "cells", axis=0, tiled=True),
        lax.all_gather(lower_local, "cells", axis=0, tiled=True),
        lax.all_gather(upper_local, "cells", axis=0, tiled=True),
        lax.all_gather(slab_residual, "cells", axis=0, tiled=True),
    )
    solved_all = lax.linalg.tridiagonal_solve(
        lower_all, main_all, upper_all, residual_all[:, None]
    )[:, 0]
    slab_fix = lax.dynamic_index_in_dim(solved_all, lax.axis_index("cells"), 0, keepdims=False)
    coarse_second = coarse_first + slab_fix
    coarse_third = (
        coarse_second
        + DAMPING
        * (coarse_rhs - coarse_apply(self_bands, lower_bands, upper_bands, coarse_second))
        / coarse_diag
    )
    lifted = prolong(slab_masks, coarse_third, layer_count, row_count, col_count)
    lifted_image = smooth_apply(pressure_coef, lifted)
    third_iterate = second_iterate + lifted - DAMPING * lifted_image / diag_fine
    pressure_fix = (
        third_iterate
        + DAMPING * (restricted - pressure_apply(pressure_coef, third_iterate)) / diag_fine
    )
    zero_field = jnp.zeros_like(pressure_fix)
    first_section = jnp.stack([pressure_fix, zero_field, zero_field])
    section_image = field_apply(jacobian, scales, first_section)
    second_rhs = krylov_basis - section_image
    direction = first_section + block_solve(jacobian, second_rhs / scales)
    image = field_apply(jacobian, scales, direction)
    along_basis = lax.psum(jnp.sum(image * krylov_basis), "cells")
    orthogonal = image - along_basis * krylov_basis
    leftover = lax.psum(jnp.sum(orthogonal * orthogonal), "cells")
    step_size = side_norm * along_basis / (along_basis * along_basis + leftover)
    return (step_size * direction, right_side - step_size * image)


def solution(mesh):
    return jax.shard_map(
        shards,
        mesh=mesh,
        in_specs=(
            P(None, None, ("groups", "cells"), None, None),
            P(None, ("groups", "cells"), None, None),
            P(None, ("groups", "cells"), None, None),
            P(None, ("groups", "cells"), None, None),
            P(("groups", "cells"), None, None),
        ),
        out_specs=(
            P(None, ("groups", "cells"), None, None),
            P(None, ("groups", "cells"), None, None),
        ),
        check_vma=False,
    )
```

profile of v0, /device:TPU:0, one launch (start us, length us, event | category | flops | bytes accessed | tf_op | source)
XLA Modules:
  0.0 911.3 jit_solution(15953883158144908310)
XLA Ops:
  2.4 35.5 %psum.21 = f32[]{:T(128)} all-reduce(f32[]{:T(128)} %multiply_reduce_fusion.2), channel_id=1, replica_groups=mesh['groups'=2,'cells'=16] {'cells'}, use_global_device_ids=true, to_apply=%region_1.2 | all-reduce | flops 1 | bytes 8 | tf_op jit(solution)/shard_map/psum | solution.py:247
  130.5 9.8 %multiply_bitcast_fusion.1 = (f32[4,4,8,8,32]{2,4,1,3,0:T(8,128)}, f32[4,4,8,8,32]{2,4,1,3,0:T(8,128)}) fusion(f32[4,8,4,32,8]{4,3,2,1,0:T(8,128)} %mul.1700, f32[4,8,4,32,8]{4,3,2,1,0:T(8,128)} %reshape.8039, f32[4,8,4,32,8]{4,3,2,1,0:T(8,128)S(1)} %copy-done.1, f32[4,8,4,32,8]{4,3,2,1,0:T(8,128)} %reshape.8038, f32[4,8,4,32,8]{4,3,2,1,0:T(8,128)S(1)} %mul.1696, ...), kind=kLoop, calls=%fused_computation.16 | loop fusion | flops 393216 | bytes 1441824 | tf_op jit(solution)/shard_map/transpose | solution.py:95
  140.3 16.8 %add_bitcast_fusion = (f32[4,4,8,8,32]{2,4,1,3,0:T(8,128)}, f32[4,4,8,8,32]{2,4,1,3,0:T(8,128)}, f32[4,4,8,8,32]{2,4,1,3,0:T(8,128)}, f32[4,4,8,8,32]{2,4,1,3,0:T(8,128)}, f32[4,4,8,8,32]{2,4,1,3,0:T(8,128)}) fusion(f32[4,8,4,32,8]{4,3,2,1,0:T(8,128)S(1)} %copy-done.2, f32[4,8,4,32,8]{4,3,2,1,0:T(8,128)} %reshape.8057, f32[4,8,4,32,8]{4,3,2,1,0:T(8,128)S(1)} %copy-done.1, ...), kind=kLoop, calls=%fused_computation.10 | loop fusion | flops 819200 | bytes 3014656 | tf_op jit(solution)/shard_map/transpose | solution.py:95
  200.5 19.2 %slice_reduce_fusion.156 = (f32[256]{0:T(256)}, f32[256]{0:T(256)}, f32[256]{0:T(256)}, f32[256]{0:T(256)}, f32[256]{0:T(256)}, /*index=5*/f32[256]{0:T(256)}, f...) fusion(f32[9,9,256]{0,1,2:T(8,128)S(1)} %convolution_bitcast_fu, ...), kind=kLoop, calls=%fused_computation.715 | loop fusion | bytes 38912 | tf_op jit(solution)/shard_map/slice | solution.py:168
  219.7 19.2 %slice_reduce_fusion.155 = (f32[256]{0:T(256)}, f32[256]{0:T(256)}, f32[256]{0:T(256)}, f32[256]{0:T(256)}, f32[256]{0:T(256)}, /*index=5*/f32[256]{0:T(256)}, f...) fusion(f32[9,9,256]{0,1,2:T(8,128)S(1)} %convolution_bitcast_fu, ...), kind=kLoop, calls=%fused_computation.714 | loop fusion | bytes 38912 | tf_op jit(solution)/shard_map/slice | solution.py:168
  239.0 19.5 %slice_reduce_fusion.154 = (f32[256]{0:T(256)}, f32[256]{0:T(256)}, f32[256]{0:T(256)}, f32[256]{0:T(256)}, f32[256]{0:T(256)}, /*index=5*/f32[256]{0:T(256)}, f...) fusion(f32[9,9,256]{0,1,2:T(8,128)S(1)} %convolution_bitcast_fu, ...), kind=kLoop, calls=%fused_computation.713 | loop fusion | bytes 38912 | tf_op jit(solution)/shard_map/slice | solution.py:168
  258.4 19.6 %slice_reduce_fusion.153 = (f32[256]{0:T(256)}, f32[256]{0:T(256)}, f32[256]{0:T(256)}, f32[256]{0:T(256)}, f32[256]{0:T(256)}, /*index=5*/f32[256]{0:T(256)}, f...) fusion(f32[9,9,256]{0,1,2:T(8,128)S(1)} %convolution_bitcast_fu, ...), kind=kLoop, calls=%fused_computation.712 | loop fusion | bytes 38912 | tf_op jit(solution)/shard_map/slice | solution.py:168
  278.0 4.8 slice_reduce_fusion.158
  295.7 19.5 %slice_reduce_fusion.72 = (f32[256]{0:T(256)}, f32[256]{0:T(256)}, f32[256]{0:T(256)}, f32[256]{0:T(256)}, f32[256]{0:T(256)}, /*index=5*/f32[256]{0:T(256)}, f3...) fusion(f32[9,9,256]{0,1,2:T(8,128)S(1)} %convolution_bitcast_fusion), kind=kLoop, calls=%fused_computation.631 | loop fusion | bytes 38912 | tf_op jit(solution)/shard_map/slice | solution.py:168
  315.2 19.5 %slice_reduce_fusion.75 = (f32[256]{0:T(256)}, f32[256]{0:T(256)}, f32[256]{0:T(256)}, f32[256]{0:T(256)}, f32[256]{0:T(256)}, /*index=5*/f32[256]{0:T(256)}, f3...) fusion(f32[9,9,256]{0,1,2:T(8,128)S(1)} %convolution_bitcast_fusion), kind=kLoop, calls=%fused_computation.634 | loop fusion | bytes 38912 | tf_op jit(solution)/shard_map/slice | solution.py:168
  334.7 19.2 %slice_reduce_fusion.74 = (f32[256]{0:T(256)}, f32[256]{0:T(256)}, f32[256]{0:T(256)}, f32[256]{0:T(256)}, f32[256]{0:T(256)}, /*index=5*/f32[256]{0:T(256)}, f3...) fusion(f32[9,9,256]{0,1,2:T(8,128)S(1)} %convolution_bitcast_fusion), kind=kLoop, calls=%fused_computation.633 | loop fusion | bytes 38912 | tf_op jit(solution)/shard_map/slice | solution.py:168
  353.9 19.6 %slice_reduce_fusion.73 = (f32[256]{0:T(256)}, f32[256]{0:T(256)}, f32[256]{0:T(256)}, f32[256]{0:T(256)}, f32[256]{0:T(256)}, /*index=5*/f32[256]{0:T(256)}, f3...) fusion(f32[9,9,256]{0,1,2:T(8,128)S(1)} %convolution_bitcast_fusion), kind=kLoop, calls=%fused_computation.632 | loop fusion | bytes 38912 | tf_op jit(solution)/shard_map/slice | solution.py:168
  373.4 4.8 slice_reduce_fusion.77
  433.4 19.0 %fusion.254 = (f32[1,128,256]{1,0,2:T(1,128)}, f32[1,128,256]{1,0,2:T(1,128)}, f32[1,128,256]{1,0,2:T(1,128)}, f32[1,128,256]{1,0,2:T(1,128)}, f32[1,128,256]{1,...) fusion(f32[1,128,256]{1,0,2:T(1,128)} %copy.265, ...), kind=kLoop, calls=%fused_computation.507 | loop fusion | flops 11567104 | bytes 3145728 | tf_op jit(solution)/shard_map/add | solution.py:158
  452.4 4.6 stack.33
  458.8 18.3 %slice_reduce_fusion.228 = (f32[256]{0:T(256)S(1)}, f32[256]{0:T(256)S(1)}, f32[256]{0:T(256)S(1)}, f32[256]{0:T(256)S(1)}, f32[256]{0:T(256)S(1)}, /*index=5*/f...) fusion(f32[9,9,256]{0,1,2:T(8,128)S(1)} %convolution_bitcast_fu, ...), kind=kLoop, calls=%fused_computation.787 | loop fusion | bytes 38912 | tf_op jit(solution)/shard_map/slice | solution.py:168
  477.1 18.6 %slice_reduce_fusion.227 = (f32[256]{0:T(256)S(1)}, f32[256]{0:T(256)S(1)}, f32[256]{0:T(256)S(1)}, f32[256]{0:T(256)S(1)}, f32[256]{0:T(256)S(1)}, /*index=5*/f...) fusion(f32[9,9,256]{0,1,2:T(8,128)S(1)} %convolution_bitcast_fu, ...), kind=kLoop, calls=%fused_computation.786 | loop fusion | bytes 38912 | tf_op jit(solution)/shard_map/slice | solution.py:168
  495.7 18.6 %slice_reduce_fusion.226 = (f32[256]{0:T(256)S(1)}, f32[256]{0:T(256)S(1)}, f32[256]{0:T(256)S(1)}, f32[256]{0:T(256)S(1)}, f32[256]{0:T(256)S(1)}, /*index=5*/f...) fusion(f32[9,9,256]{0,1,2:T(8,128)S(1)} %convolution_bitcast_fu, ...), kind=kLoop, calls=%fused_computation.785 | loop fusion | bytes 38912 | tf_op jit(solution)/shard_map/slice | solution.py:168
  514.7 19.2 %slice_reduce_fusion.225 = (f32[256]{0:T(256)S(1)}, f32[256]{0:T(256)S(1)}, f32[256]{0:T(256)S(1)}, f32[256]{0:T(256)S(1)}, f32[256]{0:T(256)S(1)}, /*index=5*/f...) fusion(f32[9,9,256]{0,1,2:T(8,128)S(1)} %convolution_bitcast_fu, ...), kind=kLoop, calls=%fused_computation.784 | loop fusion | bytes 38912 | tf_op jit(solution)/shard_map/slice | solution.py:168
  692.7 31.8 %all-reduce.243 = (f32[16]{0:T(128)S(1)}, f32[16]{0:T(128)S(1)}, f32[16]{0:T(128)S(1)}, f32[16]{0:T(128)S(1)}) all-reduce(f32[16]{0:T(128)S(1)} %dynamic-update-slice, f32[16]{0:T(128)S(1)} %dynamic-update-slice.1, f32[16]{0:T(128)S(1)} %copy-done.121, f32[16]{0:T(128)S(1)} %copy-done.119), channel_id=1, replica_groups=mesh['groups'=2,'cells'=16] {'cells'}, use_global_device_ids=true, to_apply=%add.239 | all-reduce | flops 64 | bytes 512
  794.2 8.0 select_add_fusion
  831.6 4.7 collective-permute-start.16
  842.3 32.8 %psum.22 = f32[]{:T(128)} all-reduce(f32[]{:T(128)} %multiply_reduce_fusion.1), channel_id=1, replica_groups=mesh['groups'=2,'cells'=16] {'cells'}, use_global_device_ids=true, to_apply=%region_31.32 | all-reduce | flops 1 | bytes 8 | tf_op jit(solution)/shard_map/psum | solution.py:293
  878.4 30.1 %psum.23 = f32[]{:T(128)} all-reduce(f32[]{:T(128)} %multiply_reduce_fusion), channel_id=1, replica_groups=mesh['groups'=2,'cells'=16] {'cells'}, use_global_device_ids=true, to_apply=%region_33.34 | all-reduce | flops 1 | bytes 8 | tf_op jit(solution)/shard_map/psum | solution.py:295
  (784 shorter events, 405.5 us)
Async XLA Ops:
  41.1 141.5 %copy-start.18 = (f32[4,32,256]{2,1,0:T(8,128)}, f32[4,32,256]{2,1,0:T(8,128)S(1)}, u32[]{:S(2)}) copy-start(f32[4,32,256]{2,1,0:T(8,128)S(1)} %get-tuple-element.389) | copy-start | bytes 393220
  41.8 140.8 %collective-permute-start = (f32[1,32,256]{2,1,0:T(8,128)}, f32[1,32,256]{2,1,0:T(8,128)}, u32[]{:S(2)}, u32[]{:S(2)}) collective-permute-start(f32[1,32,256]{2,1,0:T(8,128)} %get-tuple-element.464), channel_id=1, source_target_pairs={{0,1},{1,2},{2,3},{3,4},{4,5},{5,6},{6,7},{7,8},{8,9},{9,10},{10,1... | collective-permute-start | bytes 98312 | tf_op jit(solution)/shard_map/ppermute | solution.py:21
  43.7 139.0 %collective-permute-start.1 = (f32[1,32,256]{2,1,0:T(8,128)}, f32[1,32,256]{2,1,0:T(8,128)}, u32[]{:S(2)}, u32[]{:S(2)}) collective-permute-start(f32[1,32,256]{2,1,0:T(8,128)} %get-tuple-element.465), channel_id=1, source_target_pairs={{1,0},{2,1},{3,2},{4,3},{5,4},{6,5},{7,6},{8,7},{9,8},{10,9},{11,1... | collective-permute-start | bytes 98312 | tf_op jit(solution)/shard_map/ppermute | solution.py:24
  45.7 141.1 %collective-permute-start.4 = (s32[1,32,256]{2,1,0:T(8,128)}, s32[1,32,256]{2,1,0:T(8,128)}, u32[]{:S(2)}, u32[]{:S(2)}) collective-permute-start(s32[1,32,256]{2,1,0:T(8,128)} %get-tuple-element.463), channel_id=1, source_target_pairs={{0,1},{1,2},{2,3},{3,4},{4,5},{5,6},{6,7},{7,8},{8,9},{9,10},{10,1... | collective-permute-start | bytes 98312 | tf_op jit(solution)/shard_map/ppermute | solution.py:21
  49.3 137.5 %collective-permute-start.5 = (s32[1,32,256]{2,1,0:T(8,128)}, s32[1,32,256]{2,1,0:T(8,128)}, u32[]{:S(2)}, u32[]{:S(2)}) collective-permute-start(s32[1,32,256]{2,1,0:T(8,128)} %get-tuple-element.462), channel_id=1, source_target_pairs={{1,0},{2,1},{3,2},{4,3},{5,4},{6,5},{7,6},{8,7},{9,8},{10,9},{11,1... | collective-permute-start | bytes 98312 | tf_op jit(solution)/shard_map/ppermute | solution.py:24
  514.7 115.1 %copy-start.80 = (f32[256]{0:T(256)S(1)}, f32[256]{0:T(256)}, u32[]{:S(2)}) copy-start(f32[256]{0:T(256)} %get-tuple-element.173) | copy-start | bytes 3076
  514.7 115.1 %copy-start.79 = (f32[256]{0:T(256)S(1)}, f32[256]{0:T(256)}, u32[]{:S(2)}) copy-start(f32[256]{0:T(256)} %get-tuple-element.172) | copy-start | bytes 3076
  534.0 137.4 %copy-start.10 = (f32[4,32,256]{2,1,0:T(8,128)S(1)}, f32[4,32,256]{2,1,0:T(8,128)}, u32[]{:S(2)}) copy-start(f32[4,32,256]{2,1,0:T(8,128)} %get-tuple-element.386) | copy-start | bytes 393220
  534.0 137.4 %copy-start.11 = (f32[4,32,256]{2,1,0:T(8,128)S(1)}, f32[4,32,256]{2,1,0:T(8,128)}, u32[]{:S(2)}) copy-start(f32[4,32,256]{2,1,0:T(8,128)} %get-tuple-element.387) | copy-start | bytes 393220
  534.0 137.4 %copy-start.13 = (f32[4,32,256]{2,1,0:T(8,128)S(1)}, f32[4,32,256]{2,1,0:T(8,128)}, u32[]{:S(2)}) copy-start(f32[4,32,256]{2,1,0:T(8,128)} %get-tuple-element.388) | copy-start | bytes 393220
  636.4 34.4 %collective-permute-start.2 = (f32[1,32,256]{2,1,0:T(8,128)S(1)}, f32[1,32,256]{2,1,0:T(8,128)S(1)}, u32[]{:S(2)}, u32[]{:S(2)}) collective-permute-start(f32[1,32,256]{2,1,0:T(8,128)S(1)} %get-tuple-element.458), channel_id=1, source_target_pairs={{0,1},{1,2},{2,3},{3,4},{4,5},{5,6},{6,7},{7,8},{8,9},{9,10},{10,1... | collective-permute-start | bytes 98312 | tf_op jit(solution)/shard_map/ppermute | solution.py:21
  639.5 31.3 %collective-permute-start.3 = (f32[1,32,256]{2,1,0:T(8,128)S(1)}, f32[1,32,256]{2,1,0:T(8,128)S(1)}, u32[]{:S(2)}, u32[]{:S(2)}) collective-permute-start(f32[1,32,256]{2,1,0:T(8,128)S(1)} %get-tuple-element.459), channel_id=1, source_target_pairs={{1,0},{2,1},{3,2},{4,3},{5,4},{6,5},{7,6},{8,7},{9,8},{10,9},{11,1... | collective-permute-start | bytes 98312 | tf_op jit(solution)/shard_map/ppermute | solution.py:24
  678.8 10.9 %collective-permute-start.6 = (f32[1,8,32]{2,1,0:T(8,128)S(1)}, f32[1,8,32]{2,1,0:T(8,128)S(1)}, u32[]{:S(2)}, u32[]{:S(2)}) collective-permute-start(f32[1,8,32]{2,1,0:T(8,128)S(1)} %bitcast.1416), channel_id=1, source_target_pairs={{0,1},{1,2},{2,3},{3,4},{4,5},{5,6},{6,7},{7,8},{8,9},{9,10},{10,1... | collective-permute-start | bytes 3080 | tf_op jit(solution)/shard_map/ppermute | solution.py:21
  682.0 7.7 collective-permute-start.7
  778.4 4.9 collective-permute-start.8
  779.7 3.6 collective-permute-start.9
  806.4 6.0 collective-permute-start.10
  809.7 3.1 collective-permute-start.11
  813.2 5.4 collective-permute-start.12
  817.3 3.1 collective-permute-start.13
  820.8 5.7 collective-permute-start.14
  825.1 3.2 collective-permute-start.15
  831.6 6.2 collective-permute-start.16
  836.3 3.2 collective-permute-start.17
  (117 other events, 5825.4 us)
where the time goes:
time: 926 us; the launch traced here: 911 us
  local copies, waits for them, and re-layouts  531 us (57%)
  blocking collectives  130 us (14%)
  other arithmetic  122 us (13%)
  between operations  73 us (8%)
  starting transfers between devices  41.2 us (4%)
    slice x15, local copies, waits for them, and re-layouts, tile_bands(): products[own_index, delta_index].reshape(band_rows, across)  244 us
    another operation x243, local copies, waits for them, and re-layouts, tile_bands(): products[own_index, delta_index].reshape(band_rows, across)  97.7 us
    psum x1, blocking collectives, shards(): lax.psum(jnp.sum(right_side * right_side), 'cells') + 1e-06  35.5 us
    convert_element_type x14, local copies, waits for them, and re-layouts, pressure_terms(): summed = summed + weights[row_index] * scales[row_index] * jacobian[way_i...  34.9 us
    psum x1, blocking collectives, shards(): along_basis = lax.psum(jnp.sum(image * krylov_basis), 'cells')  32.8 us
    transpose x21, local copies, waits for them, and re-layouts, box_layout(): split.transpose(0, 2, 4, 1, 3)  31.9 us
    unnamed x1, blocking collectives  31.8 us
    psum x1, blocking collectives, shards(): leftover = lax.psum(jnp.sum(orthogonal * orthogonal), 'cells')  30.1 us
  transfers between devices with their start and end apart: 18, of which 4 were waited for; matrix products, arithmetic and copies ran while one was open for 17% of the time, Pallas kernels for 0%

commit v1 on v0

v1 whole, which is shorter than its diff:
```python
import functools

import jax
import jax.numpy as jnp
from jax import lax
from jax.experimental import pallas as pl
from jax.experimental.pallas import tpu as pltpu
from jax.sharding import PartitionSpec as P

AY = 4
AX = 8
DAMPING = 2.0 / 3.0
LIFT = 1024.0
F32 = jnp.float32
BF16 = jnp.bfloat16


def split_rows(x):
    hi = x.astype(BF16)
    lo = (x - hi.astype(F32)).astype(BF16)
    return jnp.concatenate([hi, lo], axis=0)


def other_box(place, width):
    part = place % width
    own = place // width
    return jnp.where(part == 0, own - 1, jnp.where(part == width - 1, own + 1, -9))


def kernel(
    n, lz, gy, gx,
    jac_hbm, side_hbm, scal_hbm, wei_hbm, ids_hbm,
    dir_hbm, img_hbm, tot_ref,
    jac, side, scal, wei, ids,
    pc, wd, rest, binv, zed, dout, iout,
    f1, f2, cf, lf, t3, pf, dr, c1, c2,
    mask, gidx, sx, sy, inv, shv,
    g0, g4, g9, g0s, g4s, g9s,
    lsem, osem, hs, hr, gs, gr,
):
    me = lax.axis_index("cells")
    has_low = me > 0
    has_high = me < n - 1
    low_id = jnp.maximum(me - 1, 0)
    high_id = jnp.minimum(me + 1, n - 1)
    top = lz - 1
    across = gx // AX
    half = gx // 2
    tiles = gy // 8

    barrier = pltpu.get_barrier_semaphore()

    @pl.loop(1, n)
    def _(step):
        pl.semaphore_signal(
            barrier, inc=1, device_id={"cells": lax.rem(me + step, n)},
            device_id_type=pl.DeviceIdType.MESH,
        )

    loads = []

    def load(src, dst):
        copy = pltpu.make_async_copy(src, dst, lsem.at[len(loads)])
        copy.start()
        loads.append(copy)
        return copy

    first_loads = [load(wei_hbm, wei), load(scal_hbm, scal)]
    first_loads += [load(jac_hbm.at[:, 3 * r], jac.at[:, 3 * r]) for r in range(3)]
    first_loads += [load(side_hbm, side)]
    ids_load = load(ids_hbm, ids)
    late_loads = [load(jac_hbm.at[:, e], jac.at[:, e]) for e in (1, 2, 4, 5, 7, 8)]

    k_row = lax.broadcasted_iota(jnp.int32, (gx, 128), 0)
    k_lane = lax.broadcasted_iota(jnp.int32, (gx, 128), 1) % across
    own = (k_row // AX == k_lane).astype(F32)
    oth = (other_box(k_row, AX) == k_lane).astype(F32)
    sx[0:gx, :] = own.astype(BF16)
    sx[gx:, :] = (oth - own).astype(BF16)
    m_row = lax.broadcasted_iota(jnp.int32, (128, 4 * gy), 0)
    m_col = lax.broadcasted_iota(jnp.int32, (128, 4 * gy), 1)
    box_row = 2 * ((m_row % 32) // 8) - 1 + m_row // 32
    grid_row = m_col % gy
    own = (grid_row // AY == box_row).astype(F32)
    oth = (other_box(grid_row, AY) == box_row).astype(F32)
    sy[...] = jnp.where((m_col // gy) % 2 == 0, own, oth - own).astype(BF16)

    zero = jnp.zeros((gy, gx), F32)

    @pl.when(jnp.logical_not(has_low))
    def _():
        for buf in (f1, f2, cf, lf, t3, pf):
            buf[0] = zero
        c1[1] = zero
        for c in range(3):
            dr[0, c] = zero

    @pl.when(jnp.logical_not(has_high))
    def _():
        for buf in (f1, f2, cf, lf, t3, pf):
            buf[lz + 1] = zero
        c1[0] = zero
        for c in range(3):
            dr[lz + 1, c] = zero

    def up_copy(e, src, dst):
        return pltpu.make_async_remote_copy(
            src_ref=src, dst_ref=dst, send_sem=hs.at[e, 0], recv_sem=hr.at[e, 0],
            device_id={"cells": high_id}, device_id_type=pl.DeviceIdType.MESH,
        )

    def down_copy(e, src, dst):
        return pltpu.make_async_remote_copy(
            src_ref=src, dst_ref=dst, send_sem=hs.at[e, 1], recv_sem=hr.at[e, 1],
            device_id={"cells": low_id}, device_id_type=pl.DeviceIdType.MESH,
        )

    pairs = []

    def exchange(up_src, up_dst, down_src, down_dst):
        e = len(pairs)
        up = up_copy(e, up_src, up_dst)
        down = down_copy(e, down_src, down_dst)
        pairs.append((up, down))

        @pl.when(has_high)
        def _():
            up.start()

        @pl.when(has_low)
        def _():
            down.start()

        def arrive():
            @pl.when(has_low)
            def _():
                up.wait_recv()

            @pl.when(has_high)
            def _():
                down.wait_recv()

        return arrive

    def halo(buf):
        return exchange(buf.at[lz], buf.at[0], buf.at[1], buf.at[lz + 1])

    groups = []

    def spread(e, src, slots):
        src_ref = src

        def copy(step):
            return pltpu.make_async_remote_copy(
                src_ref=src_ref, dst_ref=slots.at[me], send_sem=gs.at[e],
                recv_sem=gr.at[e], device_id={"cells": lax.rem(me + step, n)},
                device_id_type=pl.DeviceIdType.MESH,
            )

        @pl.loop(1, n)
        def _(step):
            copy(step).start()

        slots[me] = src[...]

        def arrive():
            pltpu.make_async_copy(
                slots.at[pl.ds(0, n - 1)], slots.at[pl.ds(0, n - 1)], gr.at[e]
            ).wait()

        def sent():
            pltpu.make_async_copy(
                slots.at[pl.ds(0, n - 1)], slots.at[pl.ds(0, n - 1)], gs.at[e]
            ).wait()

        groups.append(sent)
        return arrive

    y_at = lax.broadcasted_iota(jnp.int32, (gy, gx), 0)
    x_at = lax.broadcasted_iota(jnp.int32, (gy, gx), 1)
    in_grid = [y_at > 0, y_at < gy - 1, x_at > 0, x_at < gx - 1]

    def shifted(v, way):
        if way == 0:
            return pltpu.roll(v, 1, 0)
        if way == 1:
            return pltpu.roll(v, gy - 1, 0)
        if way == 2:
            return pltpu.roll(v, 1, 1)
        return pltpu.roll(v, gx - 1, 1)

    for copy in first_loads:
        copy.wait()

    def pressure_layer(z):
        ws = [wei[r, z] * scal[r, z] for r in range(3)]
        low_keep = jnp.where(jnp.logical_and(z == 0, me == 0), 0.0, 1.0)
        high_keep = jnp.where(jnp.logical_and(z == top, me == n - 1), 0.0, 1.0)
        for k in range(7):
            s = ws[0] * jac[k, 0, z].astype(F32)
            for r in range(1, 3):
                s = s + ws[r] * jac[k, 3 * r, z].astype(F32)
            if k == 1:
                s = s * low_keep
            if k == 2:
                s = s * high_keep
            if k >= 3:
                s = jnp.where(in_grid[k - 3], s, 0.0)
            pc[k, z] = s
            if k == 0:
                w = DAMPING / s
        rs = LIFT * (wei[0, z] * side[0, z] + wei[1, z] * side[1, z] + wei[2, z] * side[2, z])
        rest[z] = rs
        wd[z] = w
        f1[z + 1] = rs * w

    @pl.loop(0, 2)
    def _(i):
        pressure_layer(i * top)

    pl.semaphore_wait(barrier, n - 1)
    f1_in = halo(f1)

    @pl.loop(1, top)
    def _(z):
        pressure_layer(z)

    c_in = exchange(pc.at[2, top], c1.at[1], pc.at[1, 0], c1.at[0])

    def inner(buf, z):
        v = buf[z + 1]
        s = pc[0, z] * v
        for way in range(4):
            s = s + pc[3 + way, z] * shifted(v, way)
        if z > 0:
            s = s + pc[1, z] * buf[z]
        if z < top:
            s = s + pc[2, z] * buf[z + 2]
        return s

    for z in range(lz):
        f2[z + 1] = f1[z + 1] + wd[z] * (rest[z] - inner(f1, z))
    f1_in()
    f2[1] = f2[1] - wd[0] * (pc[1, 0] * f1[0])
    f2[lz] = f2[lz] - wd[top] * (pc[2, top] * f1[lz + 1])
    f2_in = halo(f2)

    row_sum = []
    main = zero
    for z in range(lz):
        s = pc[0, z] + pc[3, z] + pc[4, z] + pc[5, z] + pc[6, z]
        if z > 0:
            s = s + pc[1, z]
        if z < top:
            s = s + pc[2, z]
        row_sum.append(s)
        main = main + s
        zed[0, z] = s

    def total(v):
        s = jnp.sum(v, axis=0, keepdims=True)
        return jnp.sum(s, axis=1, keepdims=True)

    g0s[0:1, :] = jnp.broadcast_to(total(main), (1, 128))
    g0s[1:2, :] = jnp.broadcast_to(total(pc[1, 0]), (1, 128))
    g0s[2:3, :] = jnp.broadcast_to(total(pc[2, top]), (1, 128))
    g0s[3:8, :] = jnp.zeros((5, 128), F32)
    g0_in = spread(0, g0s, g0)

    ids_load.wait()
    for z in range(lz):
        a = ids[z]
        ro = (a // across != y_at // AY).astype(F32)
        co = (a % across != x_at // AX).astype(F32)
        mask[0, z] = ro
        mask[1, z] = co
        mask[2, z] = ro * co
        gidx[z] = jnp.clip(a - (2 * (y_at // 8) - 1) * across, 0, 127)

    def gathered(layers):
        t = zero
        sums = [zero, zero, zero]
        for z, v in layers:
            t = t + v
            for i in range(3):
                sums[i] = sums[i] + mask[i, z] * v
        return [t] + sums

    group_at = lax.broadcasted_iota(jnp.int32, (gy, 128), 1) // across

    def restrict(parts):
        t, ro, co, rc = parts
        stacked = jnp.concatenate(
            [jnp.concatenate([t, co], axis=1), jnp.concatenate([ro, rc], axis=1)], axis=0
        )
        out = jnp.dot(split_rows(stacked), sx[...], preferred_element_type=F32)
        out = out[: 2 * gy] + out[2 * gy :]
        out = jnp.dot(sy[...], split_rows(out), preferred_element_type=F32)
        res = out[0:gy]
        for g in range(1, 4):
            res = jnp.where(group_at == g, out[g * gy : (g + 1) * gy], res)
        return res

    def prolong(table, buf, z):
        for h in range(2):
            buf[z + 1, :, h * half : (h + 1) * half] = jnp.take_along_axis(
                table, gidx[z, :, h * half : (h + 1) * half], axis=1
            )

    def diag_layer(z):
        a = ids[z]
        s = pc[0, z]
        for way in range(4):
            s = s + jnp.where(shifted(a, way) == a, pc[3 + way, z], 0.0)
        if z > 0:
            s = s + jnp.where(ids[z - 1] == a, pc[1, z], 0.0)
        if z < top:
            s = s + jnp.where(ids[z + 1] == a, pc[2, z], 0.0)
        return s

    wdiag = DAMPING / restrict(gathered([(z, diag_layer(z)) for z in range(lz)]))

    for z in range(lz):
        zed[1, z] = rest[z] - inner(f2, z)

    f2_in()
    zed[1, 0] = zed[1, 0] - pc[1, 0] * f2[0]
    zed[1, top] = zed[1, top] - pc[2, top] * f2[lz + 1]
    rhs = restrict(gathered([(z, zed[1, z]) for z in range(lz)]))
    coarse_first = wdiag * rhs
    prolong(coarse_first, cf, 0)
    prolong(coarse_first, cf, top)
    cf_in = halo(cf)
    for z in range(1, top):
        prolong(coarse_first, cf, z)
    own_sum = zero
    for z in range(lz):
        q = zed[1, z] - inner(cf, z)
        zed[1, z] = q
        own_sum = own_sum + q
    c_in()
    lane = lax.broadcasted_iota(jnp.int32, (1, 128), 1)
    tile = jnp.where(lane == me, total(own_sum), 0.0)
    tile = tile - jnp.where(lane == me + 1, total(c1[0] * cf[lz]), 0.0)
    tile = tile - jnp.where(lane == me - 1, total(c1[1] * cf[1]), 0.0)
    g4s[...] = jnp.broadcast_to(tile, (8, 128))
    g4_in = spread(1, g4s, g4)

    g0_in()
    inv[0] = jnp.zeros((1, 128), F32)
    inv[n + 1] = jnp.zeros((1, 128), F32)
    previous_c = jnp.zeros((1, 128), F32)
    previous_d = jnp.zeros((1, 128), F32)
    for j in range(n):
        m, l, u = g0[j, 0:1, :], g0[j, 1:2, :], g0[j, 2:3, :]
        scale = 1.0 / (m - l * previous_c)
        previous_c = u * scale
        previous_d = (jnp.where(lane == j, 1.0, 0.0) - l * previous_d) * scale
        shv[j] = previous_c
        inv[j + 1] = previous_d
    for j in range(n - 2, -1, -1):
        inv[j + 1] = inv[j + 1] - shv[j] * inv[j + 2]

    row_part = restrict(gathered([(z, zed[0, z]) for z in range(lz)]))
    low_part = restrict(gathered([(0, pc[1, 0])]))
    high_part = restrict(gathered([(top, pc[2, top])]))

    cf_in()
    zed[1, 0] = zed[1, 0] - pc[1, 0] * cf[0]
    zed[1, top] = zed[1, top] - pc[2, top] * cf[lz + 1]
    rhs = restrict(gathered([(z, zed[1, z]) for z in range(lz)]))

    g4_in()
    res = g4[0, 0:1, :]
    for j in range(1, n):
        res = res + g4[j, 0:1, :]

    def fix_of(row):
        return jnp.sum(inv[row] * res, axis=1, keepdims=True)

    fix_low, fix_own, fix_high = fix_of(me), fix_of(me + 1), fix_of(me + 2)
    coarse_third = (
        coarse_first
        + fix_own
        + wdiag * (rhs - fix_own * row_part - fix_low * low_part - fix_high * high_part)
    )
    prolong(coarse_third, lf, 0)
    prolong(coarse_third, lf, top)
    lf_in = halo(lf)
    for z in range(1, top):
        prolong(coarse_third, lf, z)
    for z in range(lz):
        t3[z + 1] = f2[z + 1] + lf[z + 1] - wd[z] * inner(lf, z)
    lf_in()
    t3[1] = t3[1] - wd[0] * (pc[1, 0] * lf[0])
    t3[lz] = t3[lz] - wd[top] * (pc[2, top] * lf[lz + 1])
    t3_in = halo(t3)
    for z in range(lz):
        pf[z + 1] = t3[z + 1] + wd[z] * (rest[z] - inner(t3, z))

    for copy in late_loads:
        copy.wait()

    @pl.loop(0, lz)
    def _(z):
        mat = [jac[0, e, z].astype(F32) for e in range(9)]
        co_aa = mat[4] * mat[8] - mat[5] * mat[7]
        co_ab = mat[5] * mat[6] - mat[3] * mat[8]
        co_ac = mat[3] * mat[7] - mat[4] * mat[6]
        det = 1.0 / (mat[0] * co_aa + mat[1] * co_ab + mat[2] * co_ac)
        binv[0, z] = co_aa * det
        binv[3, z] = co_ab * det
        binv[6, z] = co_ac * det
        binv[1, z] = (mat[2] * mat[7] - mat[1] * mat[8]) * det
        binv[4, z] = (mat[0] * mat[8] - mat[2] * mat[6]) * det
        binv[7, z] = (mat[1] * mat[6] - mat[0] * mat[7]) * det
        binv[2, z] = (mat[1] * mat[5] - mat[2] * mat[4]) * det
        binv[5, z] = (mat[2] * mat[3] - mat[0] * mat[5]) * det
        binv[8, z] = (mat[0] * mat[4] - mat[1] * mat[3]) * det

    t3_in()
    pf[1] = pf[1] - wd[0] * (pc[1, 0] * t3[0])
    pf[lz] = pf[lz] - wd[top] * (pc[2, top] * t3[lz + 1])
    pf_in = halo(pf)

    def near_terms(v, way):
        return jnp.where(in_grid[way], shifted(v, way), 0.0)

    for z in range(lz):
        v = pf[z + 1]
        acc = [LIFT * side[r, z] / scal[r, z] for r in range(3)]
        for way in range(4):
            s = near_terms(v, way)
            for r in range(3):
                acc[r] = acc[r] - jac[3 + way, 3 * r, z].astype(F32) * s
        if z > 0:
            for r in range(3):
                acc[r] = acc[r] - jac[1, 3 * r, z].astype(F32) * pf[z]
        if z < top:
            for r in range(3):
                acc[r] = acc[r] - jac[2, 3 * r, z].astype(F32) * pf[z + 2]
        for r in range(3):
            zed[r, z] = acc[r]

    def solve_layer(z):
        v = [zed[r, z] for r in range(3)]
        for c in range(3):
            d = binv[3 * c, z] * v[0] + binv[3 * c + 1, z] * v[1] + binv[3 * c + 2, z] * v[2]
            dr[z + 1, c] = d
            dout[c, z] = d

    pf_in()
    for r in range(3):
        zed[r, 0] = zed[r, 0] - jac[1, 3 * r, 0].astype(F32) * pf[0]
        zed[r, top] = zed[r, top] - jac[2, 3 * r, top].astype(F32) * pf[lz + 1]
    solve_layer(0)
    solve_layer(top)
    dr_in = halo(dr)

    @pl.loop(1, top)
    def _(z):
        solve_layer(z)

    dir_out = pltpu.make_async_copy(dout, dir_hbm, osem.at[0])
    dir_out.start()

    for z in range(lz):
        acc = [zed[r, z] for r in range(3)]
        for c in range(3):
            v = dr[z + 1, c]
            for way in range(4):
                s = near_terms(v, way)
                for r in range(3):
                    acc[r] = acc[r] + jac[3 + way, 3 * r + c, z].astype(F32) * s
            if z > 0:
                for r in range(3):
                    acc[r] = acc[r] + jac[1, 3 * r + c, z].astype(F32) * dr[z, c]
            if z < top:
                for r in range(3):
                    acc[r] = acc[r] + jac[2, 3 * r + c, z].astype(F32) * dr[z + 2, c]
        for r in range(3):
            zed[r, z] = acc[r]

    dr_in()
    for c in range(3):
        for r in range(3):
            zed[r, 0] = zed[r, 0] + jac[1, 3 * r + c, 0].astype(F32) * dr[0, c]
            zed[r, top] = zed[r, top] + jac[2, 3 * r + c, top].astype(F32) * dr[lz + 1, c]
    s1, s2, s3 = zero, zero, zero
    for z in range(lz):
        for r in range(3):
            b = side[r, z]
            v = scal[r, z] * zed[r, z]
            iout[r, z] = v
            s1 = s1 + b * b
            s2 = s2 + v * (LIFT * b)
            s3 = s3 + v * v
    img_out = pltpu.make_async_copy(iout, img_hbm, osem.at[1])
    img_out.start()

    def lanes(v):
        s = v[:, :half] + v[:, half:]
        return jnp.sum(s, axis=0, keepdims=True)

    g9s[0:1, :] = lanes(s1)
    g9s[1:2, :] = lanes(s2)
    g9s[2:3, :] = lanes(s3)
    g9s[3:8, :] = jnp.zeros((5, 128), F32)
    g9_in = spread(2, g9s, g9)
    g9_in()
    tot = g9[0]
    for j in range(1, n):
        tot = tot + g9[j]
    tot_ref[...] = tot

    for up, down in pairs:
        @pl.when(has_high)
        def _(up=up):
            up.wait_send()

        @pl.when(has_low)
        def _(down=down):
            down.wait_send()

    for sent in groups:
        sent()
    dir_out.wait()
    img_out.wait()


def shards(n, jacobian, right_side, scales, weights, aggregate_of):
    lz, gy, gx = aggregate_of.shape
    field = (lz, gy, gx)
    border = (lz + 2, gy, gx)
    vm = lambda shape, dtype=F32: pltpu.VMEM(shape, dtype)
    any_spec = pl.BlockSpec(memory_space=pl.ANY)
    direction, image, totals = pl.pallas_call(
        functools.partial(kernel, n, lz, gy, gx),
        out_shape=(
            jax.ShapeDtypeStruct((3,) + field, F32),
            jax.ShapeDtypeStruct((3,) + field, F32),
            jax.ShapeDtypeStruct((8, 128), F32),
        ),
        in_specs=[any_spec] * 5,
        out_specs=(any_spec, any_spec, pl.BlockSpec(memory_space=pltpu.VMEM)),
        scratch_shapes=[
            vm((7, 9) + field, BF16), vm((3,) + field), vm((3,) + field), vm((3,) + field),
            vm(field, jnp.int32),
            vm((7,) + field), vm(field), vm(field), vm((9,) + field), vm((3,) + field),
            vm((3,) + field), vm((3,) + field),
            vm(border), vm(border), vm(border), vm(border), vm(border), vm(border),
            vm((lz + 2, 3, gy, gx)), vm((2, gy, gx)), vm((8, 128)),
            vm((3,) + field), vm(field, jnp.int32), vm((2 * gx, 128), BF16),
            vm((128, 4 * gy), BF16), vm((n + 2, 1, 128)), vm((n, 1, 128)),
            vm((n, 8, 128)), vm((n, 8, 128)), vm((n, 8, 128)),
            vm((8, 128)), vm((8, 128)), vm((8, 128)),
            pltpu.SemaphoreType.DMA((16,)), pltpu.SemaphoreType.DMA((2,)),
            pltpu.SemaphoreType.DMA((8, 2)), pltpu.SemaphoreType.DMA((8, 2)),
            pltpu.SemaphoreType.DMA((3,)), pltpu.SemaphoreType.DMA((3,)),
        ],
        compiler_params=pltpu.CompilerParams(
            collective_id=0, has_side_effects=True, vmem_limit_bytes=48 * 1024 * 1024
        ),
    )(jacobian, right_side, scales, weights, aggregate_of)
    s1, s2, s3 = (jnp.sum(totals[i]) for i in range(3))
    norm = s1 + 1e-6
    along = s2 / (LIFT * norm)
    step = s2 / (LIFT * (s3 - 1e-6 * along * along))
    return (step * direction, right_side - step * image)


def solution(mesh):
    return jax.shard_map(
        functools.partial(shards, mesh.shape["cells"]),
        mesh=mesh,
        in_specs=(
            P(None, None, ("groups", "cells"), None, None),
            P(None, ("groups", "cells"), None, None),
            P(None, ("groups", "cells"), None, None),
            P(None, ("groups", "cells"), None, None),
            P(("groups", "cells"), None, None),
        ),
        out_specs=(
            P(None, ("groups", "cells"), None, None),
            P(None, ("groups", "cells"), None, None),
        ),
        check_vma=False,
    )
```

time: 926 us -> 43.1 us (0.05); the launches traced: 911 us -> 42.8 us
  local copies, waits for them, and re-layouts: 531 us -> 3.89 us
  blocking collectives: 130 us -> 0 us
  other arithmetic: 122 us -> 1.66 us
  between operations: 73 us -> 3.35 us
  starting transfers between devices: 41.2 us -> 0 us
  Pallas kernels: 0 us -> 33.9 us
    slice x35 -> x0, local copies, waits for them, and re-layouts: 252 us -> none  [the longest x15 244 us: tile_bands(): products[own_index, delta_index].reshape(band_rows, across)]
    another operation x259 -> x0, local copies, waits for them, and re-layouts: 115 us -> none  [the longest x243 97.7 us: tile_bands(): products[own_index, delta_index].reshape(band_rows, across)]
    psum x3 -> x0, blocking collectives: 98.5 us -> none  [the longest x1 35.5 us: shards(): lax.psum(jnp.sum(right_side * right_side), 'cells') + 1e-06]
    convert_element_type x21 -> x0, local copies, waits for them, and re-layouts: 52.3 us -> none  [the longest x14 34.9 us: pressure_terms(): summed = summed + weights[row_index] * scales[row_index] * jacobian[way_i...]
    reshape x49 -> x0, local copies, waits for them, and re-layouts: 52 us -> none  [the longest x35 27.6 us: box_layout(): split.transpose(0, 2, 4, 1, 3)]
    ppermute x18 -> x0, starting transfers between devices: 41.2 us -> none  [the longest x9 29.1 us: padded_2(): lax.ppermute(lax.slice_in_dim(block, block.shape[dim] - width, None, axis...]
    pallas_call x0 -> x1, Pallas kernels: none -> 33.9 us  [shards(): pl.pallas_call(functools.partial(kernel, n, lz, gy, gx), out_shape=(jax.S...]
    transpose x21 -> x0, local copies, waits for them, and re-layouts: 31.9 us -> none  [box_layout(): split.transpose(0, 2, 4, 1, 3)]
  transfers between devices with their start and end apart: 18 -> 0, of which waited for: 4 -> 0; matrix products, arithmetic and copies ran while one was open for 17% -> 0% of each run, Pallas kernels for 0% -> 0%
where the time goes in v1:
time: 43.1 us; the launch traced here: 42.8 us
  Pallas kernels  33.9 us (79%)
  local copies, waits for them, and re-layouts  3.89 us (9%)
  between operations  3.35 us (8%)
  other arithmetic  1.66 us (4%)
    pallas_call x1, Pallas kernels, shards(): pl.pallas_call(functools.partial(kernel, n, lz, gy, gx), out_shape=(jax.S...  33.9 us
    unnamed x10, local copies, waits for them, and re-layouts  3.89 us
    sub x1, other arithmetic, shards(): return (step * direction, right_side - step * image)  0.97 us

profile of v1, /device:TPU:0, one launch (start us, length us, event | category | flops | bytes accessed | tf_op | source)
XLA Modules:
  0.0 42.8 jit_solution(9308121743554458935)
XLA Ops:
  0.6 0.0 copy-start
  0.6 1.0 %copy-done = f32[3,4,32,256]{3,2,1,0:T(8,128)S(1)} copy-done((f32[3,4,32,256]{3,2,1,0:T(8,128)S(1)}, f32[3,4,32,256]{3,2,1,0:T(8,128)}, u32[]{:S(2)}) %copy-start) | copy-done | bytes 393240
  1.6 0.0 copy-start.2
  1.6 1.0 %copy-done.2 = f32[3,4,32,256]{3,2,1,0:T(8,128)S(1)} copy-done((f32[3,4,32,256]{3,2,1,0:T(8,128)S(1)}, f32[3,4,32,256]{3,2,1,0:T(8,128)}, u32[]{:S(2)}) %copy-start.2) | copy-done | bytes 393240
  2.6 0.0 copy-start.3
  2.6 1.0 %copy-done.3 = f32[3,4,32,256]{3,2,1,0:T(8,128)S(1)} copy-done((f32[3,4,32,256]{3,2,1,0:T(8,128)S(1)}, f32[3,4,32,256]{3,2,1,0:T(8,128)}, u32[]{:S(2)}) %copy-start.3) | copy-done | bytes 393240
  3.6 0.0 copy-start.4
  3.6 0.9 %copy-done.4 = s32[4,32,256]{2,1,0:T(8,128)S(1)} copy-done((s32[4,32,256]{2,1,0:T(8,128)S(1)}, s32[4,32,256]{2,1,0:T(8,128)}, u32[]{:S(2)}) %copy-start.4) | copy-done | bytes 131096
  4.5 0.0 copy-start.1
  4.5 33.9 %shard_map.68 = (f32[3,4,32,256]{3,2,1,0:T(8,128)S(1)}, f32[3,4,32,256]{3,2,1,0:T(8,128)S(1)}, f32[8,128]{1,0:T(8,128)S(1)}) custom-call(bf16[7,9,4,32,256]{4,3,2,1,0:T(8,128)(2,1)} %jac_hbm.1, f32[3,4,32,256]{3,2,1,0:T(8,128)S(1)} %copy-done, f32[3,4,32,256]{3,2,1,0:T(8,128)S(1)} %copy-done.2, f32[3,4,32,256]{3,2,1,0:T(8,128)S(1)} %copy-done.3, ...), custom_call_target="tpu_custom_call" | custom-call | tf_op jit(solution)/shard_map/pallas_call | solution.py:537
  38.4 0.7 %slice_reduce_fusion = (f32[]{:T(128)}, f32[]{:T(128)}, f32[]{:T(128)}) fusion(f32[8,128]{1,0:T(8,128)S(1)} %get-tuple-element.5), kind=kLoop, calls=%fused_computation.2 | loop fusion | flops 381 | bytes 1548 | tf_op jit(solution)/shard_map/reduce_sum | solution.py:565
  41.8 0.0 copy-done.1
  41.8 1.0 %multiply_subtract_fusion = (f32[3,4,32,256]{3,2,1,0:T(8,128)}, f32[3,4,32,256]{3,2,1,0:T(8,128)}) fusion(f32[3,4,32,256]{3,2,1,0:T(8,128)S(1)} %copy-done.1, f32[3,4,32,256]{3,2,1,0:T(8,128)S(1)} %get-tuple-element.7, f32[]{:T(128)S(6)} %div.7, f32[3,4,32,256]{3,2,1,0:T(8,128)S(1)} %get-tuple-element.6), kind=kLoop, calls=%fused_computation | loop fusion | flops 294912 | bytes 1966084 | tf_op jit(solution)/shard_map/sub | solution.py:569
Async XLA Ops:
  0.6 1.0 %copy-start = (f32[3,4,32,256]{3,2,1,0:T(8,128)S(1)}, f32[3,4,32,256]{3,2,1,0:T(8,128)}, u32[]{:S(2)}) copy-start(f32[3,4,32,256]{3,2,1,0:T(8,128)} %side_hbm.1) | copy-start | bytes 1179652
  1.6 1.0 %copy-start.2 = (f32[3,4,32,256]{3,2,1,0:T(8,128)S(1)}, f32[3,4,32,256]{3,2,1,0:T(8,128)}, u32[]{:S(2)}) copy-start(f32[3,4,32,256]{3,2,1,0:T(8,128)} %scal_hbm.1) | copy-start | bytes 1179652
  2.6 1.0 %copy-start.3 = (f32[3,4,32,256]{3,2,1,0:T(8,128)S(1)}, f32[3,4,32,256]{3,2,1,0:T(8,128)}, u32[]{:S(2)}) copy-start(f32[3,4,32,256]{3,2,1,0:T(8,128)} %wei_hbm.1) | copy-start | bytes 1179652
  3.6 0.9 %copy-start.4 = (s32[4,32,256]{2,1,0:T(8,128)S(1)}, s32[4,32,256]{2,1,0:T(8,128)}, u32[]{:S(2)}) copy-start(s32[4,32,256]{2,1,0:T(8,128)} %ids_hbm.1) | copy-start | bytes 393220
  4.5 37.3 %copy-start.1 = (f32[3,4,32,256]{3,2,1,0:T(8,128)S(1)}, f32[3,4,32,256]{3,2,1,0:T(8,128)}, u32[]{:S(2)}) copy-start(f32[3,4,32,256]{3,2,1,0:T(8,128)} %side_hbm.1) | copy-start | bytes 1179652

commit v2 on v1

--- a/solution.py
+++ b/solution.py
@@ -30,13 +30,13 @@
 def kernel(
     n, lz, gy, gx,
     jac_hbm, side_hbm, scal_hbm, wei_hbm, ids_hbm,
-    dir_hbm, img_hbm, tot_ref,
+    dout, iout, step_ref,
     jac, side, scal, wei, ids,
-    pc, wd, rest, binv, zed, dout, iout,
-    f1, f2, cf, lf, t3, pf, dr, c1, c2,
+    pc, wd, rest, binv, zed,
+    f1, f2, cf, lf, t3, pf, dr, c1, mh, mo, f2s, t3s, drs, mm, mmh, zz,
     mask, gidx, sx, sy, inv, shv,
     g0, g4, g9, g0s, g4s, g9s,
-    lsem, osem, hs, hr, gs, gr,
+    lsem, hs, hr, gs, gr,
 ):
     me = lax.axis_index("cells")
     has_low = me > 0
@@ -92,16 +92,20 @@
         for buf in (f1, f2, cf, lf, t3, pf):
             buf[0] = zero
         c1[1] = zero
+        mh[1] = zero
         for c in range(3):
             dr[0, c] = zero
+            mmh[1, c] = zero
 
     @pl.when(jnp.logical_not(has_high))
     def _():
         for buf in (f1, f2, cf, lf, t3, pf):
             buf[lz + 1] = zero
         c1[0] = zero
+        mh[0] = zero
         for c in range(3):
             dr[lz + 1, c] = zero
+            mmh[0, c] = zero
 
     def up_copy(e, src, dst):
         return pltpu.make_async_remote_copy(
@@ -225,7 +229,15 @@
     def _(z):
         pressure_layer(z)
 
-    c_in = exchange(pc.at[2, top], c1.at[1], pc.at[1, 0], c1.at[0])
+    mo[0] = wd[0] * pc[1, 0]
+    mo[1] = wd[top] * pc[2, top]
+    m_in = exchange(mo.at[1], mh.at[1], mo.at[0], mh.at[0])
+
+    def complete(below, buf):
+        buf[1] = buf[1] - mo[0] * below[0]
+        buf[lz] = buf[lz] - mo[1] * below[lz + 1]
+        buf[0] = buf[0] - mh[1] * below[1]
+        buf[lz + 1] = buf[lz + 1] - mh[0] * below[lz]
 
     def inner(buf, z):
         v = buf[z + 1]
@@ -238,12 +250,13 @@
             s = s + pc[2, z] * buf[z + 2]
         return s
 
-    for z in range(lz):
+    for z in (0, top):
         f2[z + 1] = f1[z + 1] + wd[z] * (rest[z] - inner(f1, z))
-    f1_in()
-    f2[1] = f2[1] - wd[0] * (pc[1, 0] * f1[0])
-    f2[lz] = f2[lz] - wd[top] * (pc[2, top] * f1[lz + 1])
-    f2_in = halo(f2)
+    f2s[0] = f2[1]
+    f2s[1] = f2[lz]
+    f2_in = exchange(f2s.at[1], f2.at[0], f2s.at[0], f2.at[lz + 1])
+    for z in range(1, top):
+        f2[z + 1] = f1[z + 1] + wd[z] * (rest[z] - inner(f1, z))
 
     row_sum = []
     main = zero
@@ -266,6 +279,7 @@
     g0s[2:3, :] = jnp.broadcast_to(total(pc[2, top]), (1, 128))
     g0s[3:8, :] = jnp.zeros((5, 128), F32)
     g0_in = spread(0, g0s, g0)
+    c_in = exchange(pc.at[2, top], c1.at[1], pc.at[1, 0], c1.at[0])
 
     ids_load.wait()
     for z in range(lz):
@@ -321,9 +335,15 @@
     wdiag = DAMPING / restrict(gathered([(z, diag_layer(z)) for z in range(lz)]))
 
     for z in range(lz):
+        for r in range(3):
+            zz[r, z] = LIFT * side[r, z] / scal[r, z]
+
+    f1_in()
+    m_in()
+    f2_in()
+    complete(f1, f2)
+    for z in range(lz):
         zed[1, z] = rest[z] - inner(f2, z)
-
-    f2_in()
     zed[1, 0] = zed[1, 0] - pc[1, 0] * f2[0]
     zed[1, top] = zed[1, top] - pc[2, top] * f2[lz + 1]
     rhs = restrict(gathered([(z, zed[1, z]) for z in range(lz)]))
@@ -369,34 +389,6 @@
     zed[1, 0] = zed[1, 0] - pc[1, 0] * cf[0]
     zed[1, top] = zed[1, top] - pc[2, top] * cf[lz + 1]
     rhs = restrict(gathered([(z, zed[1, z]) for z in range(lz)]))
-
-    g4_in()
-    res = g4[0, 0:1, :]
-    for j in range(1, n):
-        res = res + g4[j, 0:1, :]
-
-    def fix_of(row):
-        return jnp.sum(inv[row] * res, axis=1, keepdims=True)
-
-    fix_low, fix_own, fix_high = fix_of(me), fix_of(me + 1), fix_of(me + 2)
-    coarse_third = (
-        coarse_first
-        + fix_own
-        + wdiag * (rhs - fix_own * row_part - fix_low * low_part - fix_high * high_part)
-    )
-    prolong(coarse_third, lf, 0)
-    prolong(coarse_third, lf, top)
-    lf_in = halo(lf)
-    for z in range(1, top):
-        prolong(coarse_third, lf, z)
-    for z in range(lz):
-        t3[z + 1] = f2[z + 1] + lf[z + 1] - wd[z] * inner(lf, z)
-    lf_in()
-    t3[1] = t3[1] - wd[0] * (pc[1, 0] * lf[0])
-    t3[lz] = t3[lz] - wd[top] * (pc[2, top] * lf[lz + 1])
-    t3_in = halo(t3)
-    for z in range(lz):
-        pf[z + 1] = t3[z + 1] + wd[z] * (rest[z] - inner(t3, z))
 
     for copy in late_loads:
         copy.wait()
@@ -418,17 +410,55 @@
         binv[5, z] = (mat[2] * mat[3] - mat[0] * mat[5]) * det
         binv[8, z] = (mat[0] * mat[4] - mat[1] * mat[3]) * det
 
+    for side_at, z, k in ((0, 0, 1), (1, top, 2)):
+        for c in range(3):
+            v = binv[3 * c, z] * jac[k, 0, z].astype(F32)
+            for r in range(1, 3):
+                v = v + binv[3 * c + r, z] * jac[k, 3 * r, z].astype(F32)
+            mm[side_at, c] = v
+    mm_in = exchange(mm.at[1], mmh.at[1], mm.at[0], mmh.at[0])
+
+    g4_in()
+    res = g4[0, 0:1, :]
+    for j in range(1, n):
+        res = res + g4[j, 0:1, :]
+
+    def fix_of(row):
+        return jnp.sum(inv[row] * res, axis=1, keepdims=True)
+
+    fix_low, fix_own, fix_high = fix_of(me), fix_of(me + 1), fix_of(me + 2)
+    coarse_third = (
+        coarse_first
+        + fix_own
+        + wdiag * (rhs - fix_own * row_part - fix_low * low_part - fix_high * high_part)
+    )
+    prolong(coarse_third, lf, 0)
+    prolong(coarse_third, lf, top)
+    lf_in = halo(lf)
+    for z in range(1, top):
+        prolong(coarse_third, lf, z)
+    for z in (0, top):
+        t3[z + 1] = f2[z + 1] + lf[z + 1] - wd[z] * inner(lf, z)
+    t3s[0] = t3[1]
+    t3s[1] = t3[lz]
+    t3_in = exchange(t3s.at[1], t3.at[0], t3s.at[0], t3.at[lz + 1])
+    for z in range(1, top):
+        t3[z + 1] = f2[z + 1] + lf[z + 1] - wd[z] * inner(lf, z)
+    lf_in()
     t3_in()
-    pf[1] = pf[1] - wd[0] * (pc[1, 0] * t3[0])
-    pf[lz] = pf[lz] - wd[top] * (pc[2, top] * t3[lz + 1])
+    complete(lf, t3)
+    for z in range(lz):
+        pf[z + 1] = t3[z + 1] + wd[z] * (rest[z] - inner(t3, z))
+    pf[1] = pf[1] - mo[0] * t3[0]
+    pf[lz] = pf[lz] - mo[1] * t3[lz + 1]
     pf_in = halo(pf)
 
     def near_terms(v, way):
         return jnp.where(in_grid[way], shifted(v, way), 0.0)
 
-    for z in range(lz):
+    def section_layer(z):
         v = pf[z + 1]
-        acc = [LIFT * side[r, z] / scal[r, z] for r in range(3)]
+        acc = [zz[r, z] for r in range(3)]
         for way in range(4):
             s = near_terms(v, way)
             for r in range(3):
@@ -447,45 +477,78 @@
         for c in range(3):
             d = binv[3 * c, z] * v[0] + binv[3 * c + 1, z] * v[1] + binv[3 * c + 2, z] * v[2]
             dr[z + 1, c] = d
-            dout[c, z] = d
-
-    pf_in()
-    for r in range(3):
-        zed[r, 0] = zed[r, 0] - jac[1, 3 * r, 0].astype(F32) * pf[0]
-        zed[r, top] = zed[r, top] - jac[2, 3 * r, top].astype(F32) * pf[lz + 1]
+
+    section_layer(0)
+    section_layer(top)
     solve_layer(0)
     solve_layer(top)
-    dr_in = halo(dr)
-
-    @pl.loop(1, top)
-    def _(z):
+    for c in range(3):
+        drs[0, c] = dr[1, c]
+        drs[1, c] = dr[lz, c]
+    dr_in = exchange(drs.at[1], dr.at[0], drs.at[0], dr.at[lz + 1])
+    for z in range(1, top):
+        section_layer(z)
+    for z in range(1, top):
         solve_layer(z)
 
-    dir_out = pltpu.make_async_copy(dout, dir_hbm, osem.at[0])
-    dir_out.start()
-
-    for z in range(lz):
-        acc = [zed[r, z] for r in range(3)]
+    def in_layer(z, acc):
         for c in range(3):
             v = dr[z + 1, c]
             for way in range(4):
                 s = near_terms(v, way)
                 for r in range(3):
                     acc[r] = acc[r] + jac[3 + way, 3 * r + c, z].astype(F32) * s
-            if z > 0:
-                for r in range(3):
-                    acc[r] = acc[r] + jac[1, 3 * r + c, z].astype(F32) * dr[z, c]
-            if z < top:
-                for r in range(3):
-                    acc[r] = acc[r] + jac[2, 3 * r + c, z].astype(F32) * dr[z + 2, c]
+        return acc
+
+    def from_layer(z, k, acc):
+        for c in range(3):
+            v = dr[z + 2 * k - 2, c]
+            for r in range(3):
+                acc[r] = acc[r] + jac[k, 3 * r + c, z].astype(F32) * v
+        return acc
+
+    def early(z):
+        acc = [zed[r, z] for r in range(3)]
+        if 0 < z < top:
+            acc = in_layer(z, acc)
+        if z > 1:
+            acc = from_layer(z, 1, acc)
+        if z < top - 1:
+            acc = from_layer(z, 2, acc)
         for r in range(3):
             zed[r, z] = acc[r]
 
+    for z in range(lz):
+        early(z)
+
+    mm_in()
+    pf_in()
+    for r in range(3):
+        zed[r, 0] = zed[r, 0] - jac[1, 3 * r, 0].astype(F32) * pf[0]
+        zed[r, top] = zed[r, top] - jac[2, 3 * r, top].astype(F32) * pf[lz + 1]
+    for c in range(3):
+        dr[1, c] = dr[1, c] - mm[0, c] * pf[0]
+        dr[lz, c] = dr[lz, c] - mm[1, c] * pf[lz + 1]
+    def late(z):
+        acc = [zed[r, z] for r in range(3)]
+        if z == 0 or z == top:
+            acc = in_layer(z, acc)
+        if z == 1:
+            acc = from_layer(z, 1, acc)
+        if z == top - 1:
+            acc = from_layer(z, 2, acc)
+        for r in range(3):
+            zed[r, z] = acc[r]
+
+    for z in range(lz):
+        late(z)
     dr_in()
     for c in range(3):
+        low = dr[0, c] - mmh[1, c] * pf[1]
+        high = dr[lz + 1, c] - mmh[0, c] * pf[lz]
         for r in range(3):
-            zed[r, 0] = zed[r, 0] + jac[1, 3 * r + c, 0].astype(F32) * dr[0, c]
-            zed[r, top] = zed[r, top] + jac[2, 3 * r + c, top].astype(F32) * dr[lz + 1, c]
+            zed[r, 0] = zed[r, 0] + jac[1, 3 * r + c, 0].astype(F32) * low
+            zed[r, top] = zed[r, top] + jac[2, 3 * r + c, top].astype(F32) * high
     s1, s2, s3 = zero, zero, zero
     for z in range(lz):
         for r in range(3):
@@ -495,8 +558,6 @@
             s1 = s1 + b * b
             s2 = s2 + v * (LIFT * b)
             s3 = s3 + v * v
-    img_out = pltpu.make_async_copy(iout, img_hbm, osem.at[1])
-    img_out.start()
 
     def lanes(v):
         s = v[:, :half] + v[:, half:]
@@ -507,11 +568,17 @@
     g9s[2:3, :] = lanes(s3)
     g9s[3:8, :] = jnp.zeros((5, 128), F32)
     g9_in = spread(2, g9s, g9)
+    for z in range(lz):
+        for c in range(3):
+            dout[c, z] = dr[z + 1, c]
     g9_in()
     tot = g9[0]
     for j in range(1, n):
         tot = tot + g9[j]
-    tot_ref[...] = tot
+    tot = jnp.sum(tot, axis=1, keepdims=True)
+    along = tot[1:2] / (LIFT * (tot[0:1] + 1e-6))
+    step = tot[1:2] / (LIFT * (tot[2:3] - 1e-6 * along * along))
+    step_ref[...] = jnp.broadcast_to(step, (gy, gx))
 
     for up, down in pairs:
         @pl.when(has_high)
@@ -524,8 +591,6 @@
 
     for sent in groups:
         sent()
-    dir_out.wait()
-    img_out.wait()
 
 
 def shards(n, jacobian, right_side, scales, weights, aggregate_of):
@@ -533,39 +598,36 @@
     field = (lz, gy, gx)
     border = (lz + 2, gy, gx)
     vm = lambda shape, dtype=F32: pltpu.VMEM(shape, dtype)
-    any_spec = pl.BlockSpec(memory_space=pl.ANY)
-    direction, image, totals = pl.pallas_call(
+    vmem_spec = pl.BlockSpec(memory_space=pltpu.VMEM)
+    direction, image, step = pl.pallas_call(
         functools.partial(kernel, n, lz, gy, gx),
         out_shape=(
             jax.ShapeDtypeStruct((3,) + field, F32),
             jax.ShapeDtypeStruct((3,) + field, F32),
-            jax.ShapeDtypeStruct((8, 128), F32),
+            jax.ShapeDtypeStruct((gy, gx), F32),
         ),
-        in_specs=[any_spec] * 5,
-        out_specs=(any_spec, any_spec, pl.BlockSpec(memory_space=pltpu.VMEM)),
+        in_specs=[pl.BlockSpec(memory_space=pltpu.HBM)] * 5,
+        out_specs=(vmem_spec,) * 3,
         scratch_shapes=[
             vm((7, 9) + field, BF16), vm((3,) + field), vm((3,) + field), vm((3,) + field),
             vm(field, jnp.int32),
             vm((7,) + field), vm(field), vm(field), vm((9,) + field), vm((3,) + field),
-            vm((3,) + field), vm((3,) + field),
             vm(border), vm(border), vm(border), vm(border), vm(border), vm(border),
-            vm((lz + 2, 3, gy, gx)), vm((2, gy, gx)), vm((8, 128)),
+            vm((lz + 2, 3, gy, gx)), vm((2, gy, gx)), vm((2, gy, gx)), vm((2, gy, gx)),
+            vm((2, gy, gx)), vm((2, gy, gx)), vm((2, 3, gy, gx)), vm((2, 3, gy, gx)),
+            vm((2, 3, gy, gx)), vm((3,) + field),
             vm((3,) + field), vm(field, jnp.int32), vm((2 * gx, 128), BF16),
             vm((128, 4 * gy), BF16), vm((n + 2, 1, 128)), vm((n, 1, 128)),
             vm((n, 8, 128)), vm((n, 8, 128)), vm((n, 8, 128)),
             vm((8, 128)), vm((8, 128)), vm((8, 128)),
-            pltpu.SemaphoreType.DMA((16,)), pltpu.SemaphoreType.DMA((2,)),
-            pltpu.SemaphoreType.DMA((8, 2)), pltpu.SemaphoreType.DMA((8, 2)),
+            pltpu.SemaphoreType.DMA((16,)),
+            pltpu.SemaphoreType.DMA((12, 2)), pltpu.SemaphoreType.DMA((12, 2)),
             pltpu.SemaphoreType.DMA((3,)), pltpu.SemaphoreType.DMA((3,)),
         ],
         compiler_params=pltpu.CompilerParams(
-            collective_id=0, has_side_effects=True, vmem_limit_bytes=48 * 1024 * 1024
+            collective_id=0, has_side_effects=True, vmem_limit_bytes=54 * 1024 * 1024
         ),
     )(jacobian, right_side, scales, weights, aggregate_of)
-    s1, s2, s3 = (jnp.sum(totals[i]) for i in range(3))
-    norm = s1 + 1e-6
-    along = s2 / (LIFT * norm)
-    step = s2 / (LIFT * (s3 - 1e-6 * along * along))
     return (step * direction, right_side - step * image)
 
 

time: 43.1 us -> 32.7 us (0.76)
  Pallas kernels: 33.9 us -> 29.7 us
  local copies, waits for them, and re-layouts: 3.89 us -> 0.01 us
  between operations: 3.35 us -> 0.65 us
  other arithmetic: 1.66 us -> 2.13 us
    pallas_call x1, Pallas kernels: 33.9 us -> 29.7 us  [shards(): pl.pallas_call(functools.partial(kernel, n, lz, gy, gx), out_shape=(jax.S...]
    unnamed x10 -> x2, local copies, waits for them, and re-layouts: 3.89 us -> 0.01 us
    sub x1, other arithmetic: 0.97 us -> 2.13 us  [shards(): return (step * direction, right_side - step * image)]
    reduce_sum x1 -> x0, other arithmetic: 0.69 us -> none  [shards(): s1, s2, s3 = (jnp.sum(totals[i]) for i in range(3))]
where the time goes in v2:
time: 32.7 us; the launch traced here: 32.5 us
  Pallas kernels  29.7 us (91%)
  other arithmetic  2.13 us (7%)
  between operations  0.65 us (2%)
    pallas_call x1, Pallas kernels, shards(): pl.pallas_call(functools.partial(kernel, n, lz, gy, gx), out_shape=(jax.S...  29.7 us
    sub x1, other arithmetic, shards(): return (step * direction, right_side - step * image)  2.13 us

profile of v2, /device:TPU:0, one launch (start us, length us, event | category | flops | bytes accessed | tf_op | source)
XLA Modules:
  0.0 32.5 jit_solution(15556151417301474167)
XLA Ops:
  0.6 0.0 copy-start
  0.6 29.7 %shard_map.68 = (f32[3,4,32,256]{3,2,1,0:T(8,128)}, f32[3,4,32,256]{3,2,1,0:T(8,128)}, f32[32,256]{1,0:T(8,128)}) custom-call(bf16[7,9,4,32,256]{4,3,2,1,0:T(8,128)(2,1)} %jac_hbm.1, f32[3,4,32,256]{3,2,1,0:T(8,128)} %side_hbm.1, f32[3,4,32,256]{3,2,1,0:T(8,128)} %scal_hbm.1, f32[3,4,32,256]{3,2,1,0:T(8,128)} %wei_hbm.1, s32[4,32,256]{2,1,0:T(8,128)} %ids_hbm.1), custom_call_target="tpu_custom_call" | custom-call | tf_op jit(solution)/shard_map/pallas_call | solution.py:602
  30.4 0.0 copy-done
  30.4 2.1 %multiply_subtract_fusion = (f32[3,4,32,256]{3,2,1,0:T(8,128)}, f32[3,4,32,256]{3,2,1,0:T(8,128)}) fusion(f32[3,4,32,256]{3,2,1,0:T(8,128)S(1)} %copy-done, f32[3,4,32,256]{3,2,1,0:T(8,128)} %get-tuple-element.7, f32[32,256]{1,0:T(8,128)} %get-tuple-element.5, f32[3,4,32,256]{3,2,1,0:T(8,128)} %get-tuple-element.6), kind=kLoop, calls=%fused_computation | loop fusion | flops 294912 | bytes 1998848 | tf_op jit(solution)/shard_map/sub | solution.py:631
Async XLA Ops:
  0.6 29.7 %copy-start = (f32[3,4,32,256]{3,2,1,0:T(8,128)S(1)}, f32[3,4,32,256]{3,2,1,0:T(8,128)}, u32[]{:S(2)}) copy-start(f32[3,4,32,256]{3,2,1,0:T(8,128)} %side_hbm.1) | copy-start | bytes 1179652

commit v3 on v2

--- a/solution.py
+++ b/solution.py
@@ -30,13 +30,13 @@
 def kernel(
     n, lz, gy, gx,
     jac_hbm, side_hbm, scal_hbm, wei_hbm, ids_hbm,
-    dout, iout, step_ref,
+    dir_hbm, img_hbm, step_ref,
     jac, side, scal, wei, ids,
-    pc, wd, rest, binv, zed,
+    pc, wd, rest, binv, zed, dout, iout,
     f1, f2, cf, lf, t3, pf, dr, c1, mh, mo, f2s, t3s, drs, mm, mmh, zz,
     mask, gidx, sx, sy, inv, shv,
     g0, g4, g9, g0s, g4s, g9s,
-    lsem, hs, hr, gs, gr,
+    lsem, osem, hs, hr, gs, gr,
 ):
     me = lax.axis_index("cells")
     has_low = me > 0
@@ -541,6 +541,11 @@
             zed[r, z] = acc[r]
 
     for z in range(lz):
+        for c in range(3):
+            dout[c, z] = dr[z + 1, c]
+    dir_out = pltpu.make_async_copy(dout, dir_hbm, osem.at[0])
+    dir_out.start()
+    for z in range(lz):
         late(z)
     dr_in()
     for c in range(3):
@@ -559,6 +564,9 @@
             s2 = s2 + v * (LIFT * b)
             s3 = s3 + v * v
 
+    img_out = pltpu.make_async_copy(iout, img_hbm, osem.at[1])
+    img_out.start()
+
     def lanes(v):
         s = v[:, :half] + v[:, half:]
         return jnp.sum(s, axis=0, keepdims=True)
@@ -568,9 +576,6 @@
     g9s[2:3, :] = lanes(s3)
     g9s[3:8, :] = jnp.zeros((5, 128), F32)
     g9_in = spread(2, g9s, g9)
-    for z in range(lz):
-        for c in range(3):
-            dout[c, z] = dr[z + 1, c]
     g9_in()
     tot = g9[0]
     for j in range(1, n):
@@ -591,6 +596,8 @@
 
     for sent in groups:
         sent()
+    dir_out.wait()
+    img_out.wait()
 
 
 def shards(n, jacobian, right_side, scales, weights, aggregate_of):
@@ -598,6 +605,7 @@
     field = (lz, gy, gx)
     border = (lz + 2, gy, gx)
     vm = lambda shape, dtype=F32: pltpu.VMEM(shape, dtype)
+    any_spec = pl.BlockSpec(memory_space=pl.ANY)
     vmem_spec = pl.BlockSpec(memory_space=pltpu.VMEM)
     direction, image, step = pl.pallas_call(
         functools.partial(kernel, n, lz, gy, gx),
@@ -607,11 +615,12 @@
             jax.ShapeDtypeStruct((gy, gx), F32),
         ),
         in_specs=[pl.BlockSpec(memory_space=pltpu.HBM)] * 5,
-        out_specs=(vmem_spec,) * 3,
+        out_specs=(any_spec, any_spec, vmem_spec),
         scratch_shapes=[
             vm((7, 9) + field, BF16), vm((3,) + field), vm((3,) + field), vm((3,) + field),
             vm(field, jnp.int32),
             vm((7,) + field), vm(field), vm(field), vm((9,) + field), vm((3,) + field),
+            vm((3,) + field), vm((3,) + field),
             vm(border), vm(border), vm(border), vm(border), vm(border), vm(border),
             vm((lz + 2, 3, gy, gx)), vm((2, gy, gx)), vm((2, gy, gx)), vm((2, gy, gx)),
             vm((2, gy, gx)), vm((2, gy, gx)), vm((2, 3, gy, gx)), vm((2, 3, gy, gx)),
@@ -620,12 +629,12 @@
             vm((128, 4 * gy), BF16), vm((n + 2, 1, 128)), vm((n, 1, 128)),
             vm((n, 8, 128)), vm((n, 8, 128)), vm((n, 8, 128)),
             vm((8, 128)), vm((8, 128)), vm((8, 128)),
-            pltpu.SemaphoreType.DMA((16,)),
+            pltpu.SemaphoreType.DMA((16,)), pltpu.SemaphoreType.DMA((2,)),
             pltpu.SemaphoreType.DMA((12, 2)), pltpu.SemaphoreType.DMA((12, 2)),
             pltpu.SemaphoreType.DMA((3,)), pltpu.SemaphoreType.DMA((3,)),
         ],
         compiler_params=pltpu.CompilerParams(
-            collective_id=0, has_side_effects=True, vmem_limit_bytes=54 * 1024 * 1024
+            collective_id=0, has_side_effects=True, vmem_limit_bytes=60 * 1024 * 1024
         ),
     )(jacobian, right_side, scales, weights, aggregate_of)
     return (step * direction, right_side - step * image)

time: 32.7 us -> 32.4 us (level)
  no operation moved by 1% of the time
where the time goes in v3:
time: 32.4 us; the launch traced here: 32.2 us
  Pallas kernels  29.5 us (91%)
  other arithmetic  2.13 us (7%)
  between operations  0.65 us (2%)
    pallas_call x1, Pallas kernels, shards(): pl.pallas_call(functools.partial(kernel, n, lz, gy, gx), out_shape=(jax.S...  29.5 us
    sub x1, other arithmetic, shards(): return (step * direction, right_side - step * image)  2.13 us

profile of v3, /device:TPU:0, one launch (start us, length us, event | category | flops | bytes accessed | tf_op | source)
XLA Modules:
  0.0 32.2 jit_solution(4719297131523748757)
XLA Ops:
  0.6 0.0 copy-start
  0.6 29.5 %shard_map.68 = (f32[3,4,32,256]{3,2,1,0:T(8,128)}, f32[3,4,32,256]{3,2,1,0:T(8,128)}, f32[32,256]{1,0:T(8,128)}) custom-call(bf16[7,9,4,32,256]{4,3,2,1,0:T(8,128)(2,1)} %jac_hbm.1, f32[3,4,32,256]{3,2,1,0:T(8,128)} %side_hbm.1, f32[3,4,32,256]{3,2,1,0:T(8,128)} %scal_hbm.1, f32[3,4,32,256]{3,2,1,0:T(8,128)} %wei_hbm.1, s32[4,32,256]{2,1,0:T(8,128)} %ids_hbm.1), custom_call_target="tpu_custom_call" | custom-call | tf_op jit(solution)/shard_map/pallas_call | solution.py:610
  30.1 0.0 copy-done
  30.1 2.1 %multiply_subtract_fusion = (f32[3,4,32,256]{3,2,1,0:T(8,128)}, f32[3,4,32,256]{3,2,1,0:T(8,128)}) fusion(f32[3,4,32,256]{3,2,1,0:T(8,128)S(1)} %copy-done, f32[3,4,32,256]{3,2,1,0:T(8,128)} %get-tuple-element.7, f32[32,256]{1,0:T(8,128)} %get-tuple-element.5, f32[3,4,32,256]{3,2,1,0:T(8,128)} %get-tuple-element.6), kind=kLoop, calls=%fused_computation | loop fusion | flops 294912 | bytes 1998848 | tf_op jit(solution)/shard_map/sub | solution.py:640
Async XLA Ops:
  0.6 29.5 %copy-start = (f32[3,4,32,256]{3,2,1,0:T(8,128)S(1)}, f32[3,4,32,256]{3,2,1,0:T(8,128)}, u32[]{:S(2)}) copy-start(f32[3,4,32,256]{3,2,1,0:T(8,128)} %side_hbm.1) | copy-start | bytes 1179652

commit v4 on v3

--- a/solution.py
+++ b/solution.py
@@ -161,8 +161,7 @@
                 device_id_type=pl.DeviceIdType.MESH,
             )
 
-        @pl.loop(1, n)
-        def _(step):
+        for step in range(1, n):
             copy(step).start()
 
         slots[me] = src[...]
@@ -338,6 +337,16 @@
         for r in range(3):
             zz[r, z] = LIFT * side[r, z] / scal[r, z]
 
+    for z in range(lz):
+        s = pc[0, z]
+        for way in range(4):
+            s = s + shifted(pc[3 + way, z], way ^ 1)
+        if z < top:
+            s = s + pc[1, z + 1]
+        if z > 0:
+            s = s + pc[2, z - 1]
+        zed[2, z] = s
+
     f1_in()
     m_in()
     f2_in()
@@ -355,9 +364,7 @@
         prolong(coarse_first, cf, z)
     own_sum = zero
     for z in range(lz):
-        q = zed[1, z] - inner(cf, z)
-        zed[1, z] = q
-        own_sum = own_sum + q
+        own_sum = own_sum + (zed[1, z] - zed[2, z] * cf[z + 1])
     c_in()
     lane = lax.broadcasted_iota(jnp.int32, (1, 128), 1)
     tile = jnp.where(lane == me, total(own_sum), 0.0)
@@ -365,6 +372,8 @@
     tile = tile - jnp.where(lane == me - 1, total(c1[1] * cf[1]), 0.0)
     g4s[...] = jnp.broadcast_to(tile, (8, 128))
     g4_in = spread(1, g4s, g4)
+    for z in range(lz):
+        zed[1, z] = zed[1, z] - inner(cf, z)
 
     g0_in()
     inv[0] = jnp.zeros((1, 128), F32)

time: 32.4 us -> 32.3 us (level)
  no operation moved by 1% of the time
where the time goes in v4:
time: 32.3 us; the launch traced here: 32.2 us
  Pallas kernels  29.4 us (91%)
  other arithmetic  2.13 us (7%)
  between operations  0.65 us (2%)
    pallas_call x1, Pallas kernels, shards(): pl.pallas_call(functools.partial(kernel, n, lz, gy, gx), out_shape=(jax.S...  29.4 us
    sub x1, other arithmetic, shards(): return (step * direction, right_side - step * image)  2.13 us

profile of v4, /device:TPU:0, one launch (start us, length us, event | category | flops | bytes accessed | tf_op | source)
XLA Modules:
  0.0 32.2 jit_solution(16231085779033317274)
XLA Ops:
  0.6 0.0 copy-start
  0.6 29.4 %shard_map.68 = (f32[3,4,32,256]{3,2,1,0:T(8,128)}, f32[3,4,32,256]{3,2,1,0:T(8,128)}, f32[32,256]{1,0:T(8,128)}) custom-call(bf16[7,9,4,32,256]{4,3,2,1,0:T(8,128)(2,1)} %jac_hbm.1, f32[3,4,32,256]{3,2,1,0:T(8,128)} %side_hbm.1, f32[3,4,32,256]{3,2,1,0:T(8,128)} %scal_hbm.1, f32[3,4,32,256]{3,2,1,0:T(8,128)} %wei_hbm.1, s32[4,32,256]{2,1,0:T(8,128)} %ids_hbm.1), custom_call_target="tpu_custom_call" | custom-call | tf_op jit(solution)/shard_map/pallas_call | solution.py:619
  30.0 0.0 copy-done
  30.1 2.1 %multiply_subtract_fusion = (f32[3,4,32,256]{3,2,1,0:T(8,128)}, f32[3,4,32,256]{3,2,1,0:T(8,128)}) fusion(f32[3,4,32,256]{3,2,1,0:T(8,128)S(1)} %copy-done, f32[3,4,32,256]{3,2,1,0:T(8,128)} %get-tuple-element.7, f32[32,256]{1,0:T(8,128)} %get-tuple-element.5, f32[3,4,32,256]{3,2,1,0:T(8,128)} %get-tuple-element.6), kind=kLoop, calls=%fused_computation | loop fusion | flops 294912 | bytes 1998848 | tf_op jit(solution)/shard_map/sub | solution.py:649
Async XLA Ops:
  0.6 29.4 %copy-start = (f32[3,4,32,256]{3,2,1,0:T(8,128)S(1)}, f32[3,4,32,256]{3,2,1,0:T(8,128)}, u32[]{:S(2)}) copy-start(f32[3,4,32,256]{3,2,1,0:T(8,128)} %side_hbm.1) | copy-start | bytes 1179652
